TPU v7x, 32 devices: a whole 2x2x4 slice. The times are simulated.
32 devices in a mesh: parts: 2 (over x), wide: 16 (over z, y, core).
Axes of the slice: x: 2, y: 2, z: 4, core: 2. Of those that a mesh axis runs over, the one named last changes fastest.
Arguments:
- hidden_grads: bfloat16 [512, 14784], P(('parts', 'wide')), parts along dimension 0, may hold values from -400 to 400
- tile_slot: int32 [156], P('parts'), parts along dimension 0, may hold values from 0 to 79, as said below
Outputs:
- factor_tiles: float32 [160, 1232, 1232], P(('parts', 'wide')), parts along dimension 0
There are 2 independent parts, one for each index of `parts`. A program takes and returns all parts, laid end to end along the dimension named above; each array names one. Nothing has to cross between parts.
Inputs may be any that keep to these rules, and one draw needn't show every extreme that they name: `tile_slot`: entries are distinct. The device of slot s is s // 5; some device owns exactly 5 tiles.
All inputs are finite; a program needn't handle non-finite values.
Results may differ from a plain program's by a relative error of at most 0.0003.
Values may be sent and summed in bfloat16 or wider, within the bound.
A program may use at most 128 MiB of HBM per device.

v0:
```python
import jax
import jax.numpy as jnp
import numpy as np
from jax import lax
from jax.sharding import PartitionSpec as P

FF = 14784
P_SIZE = 1232
NP = 12
TILES = 78


DAMPING = 0.1


def pair_grams(left_cols, right_cols):
    return jnp.einsum("tkp,tkq->kpq", left_cols, right_cols, preferred_element_type=jnp.float32)


def slot_grams(arrived):
    return pair_grams(arrived[:, 0, :, :P_SIZE], arrived[:, 0, :, P_SIZE:])


def build_outgoing(hidden_grads, left_panel, right_panel, wide_count, slot_count):
    tok_rows = hidden_grads.shape[0]
    by_panel = hidden_grads.reshape(tok_rows, NP, P_SIZE)
    panel_index = jnp.stack([left_panel, right_panel], axis=1).reshape(-1)
    chosen_cols = jnp.take(by_panel, panel_index, axis=1)
    return chosen_cols.reshape(tok_rows, wide_count, slot_count, 2 * P_SIZE)


def shards(hidden_grads, tile_slot):
    wide_count = lax.axis_size("wide")
    slot_count = (TILES + wide_count - 1) // wide_count
    capacity = wide_count * slot_count
    my_index = lax.axis_index("wide")
    local_squares = jnp.sum(jnp.square(hidden_grads.astype(jnp.float32)))
    square_sum = lax.psum(local_squares, "wide")
    upper_rows, upper_cols = np.triu_indices(NP)
    row_table = jnp.asarray(upper_rows, jnp.int32)
    col_table = jnp.asarray(upper_cols, jnp.int32)
    slot_match = tile_slot[None, :] == jnp.arange(capacity, dtype=jnp.int32)[:, None]
    slot_used = jnp.any(slot_match, axis=1)
    left_panel = jnp.sum(jnp.where(slot_match, row_table[None, :], 0), axis=1)
    right_panel = jnp.sum(jnp.where(slot_match, col_table[None, :], 0), axis=1)
    first_slot = my_index * slot_count
    my_left = lax.dynamic_slice_in_dim(left_panel, first_slot, slot_count)
    my_right = lax.dynamic_slice_in_dim(right_panel, first_slot, slot_count)
    my_used = lax.dynamic_slice_in_dim(slot_used, first_slot, slot_count)
    outgoing = build_outgoing(hidden_grads, left_panel, right_panel, wide_count, slot_count)
    products = slot_grams(lax.all_to_all(outgoing, "wide", split_axis=1, concat_axis=0, tiled=True))
    diag_slot = ((my_left == my_right) & my_used).astype(jnp.float32)
    identity_tile = jnp.eye(P_SIZE, dtype=jnp.float32)
    factor = products * (FF / square_sum) + DAMPING * identity_tile[None] * diag_slot[:, None, None]
    return jnp.where(my_used[:, None, None], factor, 0.0)


def solution(mesh):
    in_specs = (P(("parts", "wide"), None), P("parts"))
    out_specs = P(("parts", "wide"), None, None)
    return jax.shard_map(shards, mesh=mesh, in_specs=in_specs, out_specs=out_specs, check_vma=False)
```

profile of v0, /device:TPU:18, one launch (start us, length us, event | category | flops | bytes accessed | tf_op | source)
XLA Modules:
  0.0 254.7 jit_solution(10512844550040891953)
XLA Ops:
  0.0 0.8 select_reduce_fusion.1
  0.8 0.1 stack.15
  0.9 0.1 copy.32
  1.0 0.1 stack.16
  1.1 0.1 copy.33
  1.2 0.1 copy.34
  1.3 0.1 copy.36
  1.4 0.1 reshape.65
  1.6 0.3 broadcast_in_dim.55
  1.9 0.4 broadcast_in_dim.56
  2.3 0.2 copy.35
  2.5 2.0 reshape.64
  4.5 0.1 copy.37
  4.6 8.8 %gather_fusion = bf16[160,16,1232]{2,1,0:T(8,128)(2,1)} fusion(bf16[16,12,1232]{2,0,1:T(8,128)(2,1)S(1)} %copy.37, s32[1024]{0:T(1024)S(1)} %pad_clamp_fusion), kind=kCustom, calls=%fused_computation | custom fusion | bytes 12616320 | tf_op jit(solution)/shard_map/jit(_take)/gather | solution.py:28
  13.4 7.7 %copy.38 = bf16[16,160,1232]{2,1,0:T(8,128)(2,1)} copy(bf16[16,160,1232]{2,0,1:T(8,128)(2,1)} %bitcast.19) | data formatting | bytes 12615680 | tf_op jit(solution)/shard_map/jit(_take)/gather | solution.py:28
  21.1 15.5 %gather.7 = bf16[16,16,5,2464]{3,2,1,0:T(8,128)(2,1)} reshape(bf16[16,160,1232]{2,1,0:T(8,128)(2,1)} %copy.38) | data formatting | bytes 12615680 | tf_op jit(solution)/shard_map/jit(_take)/gather | solution.py:28
  36.7 10.1 %broadcast_select_fusion = bf16[16,16,5,2464]{3,2,1,0:T(8,128)(2,1)} fusion(bf16[16,16,5,2464]{3,2,1,0:T(8,128)(2,1)} %gather.7, pred[16,5,2464]{2,1,0:T(8,128)(4,1)S(1)} %copy.35), kind=kLoop, calls=%fused_computation.4 | loop fusion | flops 3153920 | bytes 12812800 | tf_op jit(solution)/shard_map/jit(_take)/select_n | solution.py:28
  46.8 10.9 %copy.39 = bf16[16,16,5,2464]{3,0,2,1:T(8,128)(2,1)} copy(bf16[16,16,5,2464]{3,2,1,0:T(8,128)(2,1)} %broadcast_select_fusion) | data formatting | bytes 12615680 | tf_op jit(solution)/shard_map/jit(_take)/select_n | solution.py:28
  57.7 0.0 copy-start
  57.7 0.0 copy-start.1
  57.7 6.3 %all-to-all-start = ((bf16[16,16,5,2464]{3,0,2,1:T(8,128)(2,1)}), bf16[16,16,5,2464]{3,0,2,1:T(8,128)(2,1)}, u32[]{:S(2)}, u32[]{:S(2)}) async-start(bf16[16,16,5,2464]{3,0,2,1:T(8,128)(2,1)} %copy.39), calls=%async_computation | async-start | bytes 13107200 | tf_op jit(solution)/shard_map/all_to_all | solution.py:51
  64.0 0.0 copy-done
  64.0 0.8 multiply_reduce_fusion
  64.9 161.0 %psum.7 = f32[]{:T(128)} all-reduce(f32[]{:T(128)} %multiply_reduce_fusion), channel_id=1, replica_groups=mesh['parts'=2,'wide'=16] {'wide'}, use_global_device_ids=true, to_apply=%region_4.5 | all-reduce | flops 1 | bytes 8 | tf_op jit(solution)/shard_map/psum | solution.py:38
  226.6 0.0 copy-done.1
  226.6 0.1 fusion.3
  226.7 0.1 and_convert_fusion
  226.8 3.0 %fusion.2 = f32[1232,1232]{1,0:T(8,128)} fusion(), kind=kLoop, calls=%fused_computation.6 | loop fusion | flops 3035648 | bytes 6071296 | tf_op jit(solution)/shard_map/mul | solution.py:54
  229.9 0.0 all-to-all-done
  229.9 6.1 %copy.40 = bf16[16,16,1,5,2464]{4,1,0,3,2:T(8,128)(2,1)} copy(bf16[16,16,1,5,2464]{4,1,3,0,2:T(8,128)(2,1)} %bitcast.5) | data formatting | bytes 12615680 | tf_op jit(solution)/shard_map/all_to_all | solution.py:51
  236.0 18.8 %fusion.1 = f32[5,1232,1232]{2,1,0:T(8,128)} fusion(f32[5]{0:T(128)S(1)} %get-tuple-element.7, f32[1232,1232]{1,0:T(8,128)} %fusion.2, f32[]{:T(128)S(6)} %div.3, pred[5]{0:T(512)(128)(4,1)S(1)} %get-tuple-element.8, bf16[256,1,5,2464]{3,0,2,1:T(8,128)(2,1)} %bitcast.18), kind=kOutput, calls=%fused_computation.3 | convolution fusion | flops 3915985920 | bytes 42735644 | tf_op jit(solution)/shard_map/tkp,tkq->kpq/dot_general | solution.py:17
  (4 shorter events, 0.1 us)
Async XLA Ops:
  57.7 6.3 %copy-start = (bf16[16,14784]{1,0:T(8,128)(2,1)S(1)}, bf16[16,14784]{1,0:T(8,128)(2,1)}, u32[]{:S(2)}) copy-start(bf16[16,14784]{1,0:T(8,128)(2,1)} %param.4) | copy-start | bytes 1419268
  57.7 168.9 %copy-start.1 = (s32[78]{0:T(128)S(1)}, s32[78]{0:T(128)}, u32[]{:S(2)}) copy-start(s32[78]{0:T(128)} %param.5) | copy-start | bytes 940
  57.7 172.1 %all-to-all-start = ((bf16[16,16,5,2464]{3,0,2,1:T(8,128)(2,1)}), bf16[16,16,5,2464]{3,0,2,1:T(8,128)(2,1)}, u32[]{:S(2)}, u32[]{:S(2)}) async-start(bf16[16,16,5,2464]{3,0,2,1:T(8,128)(2,1)} %copy.39), calls=%async_computation | async-start | bytes 13107200 | tf_op jit(solution)/shard_map/all_to_all | solution.py:51
where the time goes:
time: 256 us; the launch traced here: 255 us
  blocking collectives  161 us (63%)
  local copies, waits for them, and re-layouts  52.8 us (21%)
  matrix products  18.8 us (7%)
  other arithmetic  15 us (6%)
  starting transfers between devices  6.32 us (2%)
    psum x1, blocking collectives, shards(): square_sum = lax.psum(local_squares, 'wide')  161 us
    gather x3, local copies, waits for them, and re-layouts, build_outgoing(): chosen_cols = jnp.take(by_panel, panel_index, axis=1)  32 us
    dot_general x1, matrix products, pair_grams(): jnp.einsum('tkp,tkq->kpq', left_cols, right_cols, preferred_element_type=...  18.8 us
    select_n x1, local copies, waits for them, and re-layouts, build_outgoing(): chosen_cols = jnp.take(by_panel, panel_index, axis=1)  10.9 us
    select_n x2, other arithmetic, build_outgoing(): chosen_cols = jnp.take(by_panel, panel_index, axis=1)  10.1 us
    all_to_all x1, starting transfers between devices, shards(): lax.all_to_all(outgoing, 'wide', split_axis=1, concat_axis=0, tiled=True)  6.32 us
    all_to_all x1, local copies, waits for them, and re-layouts, shards(): lax.all_to_all(outgoing, 'wide', split_axis=1, concat_axis=0, tiled=True)  6.12 us
  transfers between devices with their start and end apart: 1, of which 0 were waited for; matrix products, arithmetic and copies ran while one was open for 2% of the time, Pallas kernels for 0%

commit v1 on v0

v1 whole, which is shorter than its diff:
```python
import functools

import jax
import jax.numpy as jnp
import numpy as np
from jax import lax
from jax.experimental import pallas as pl
from jax.experimental.pallas import tpu as pltpu
from jax.sharding import PartitionSpec as P

FF = 14784
P_SIZE = 1232
NP = 12
TILES = 78
DAMPING = 0.1

P_PAD = 1280
CHUNKS = 4
CHUNK_PANELS = NP // CHUNKS
ROW_BLOCK = 256
MESH = pl.DeviceIdType.MESH


def ring_position(chip, chips):
    if chips != 8:
        return chip
    depth, side = chip // 2, chip % 2
    return depth + side * (chips - 1 - 2 * depth)


def ring_chip(position, chips):
    if chips != 8:
        return position
    side = position // (chips // 2)
    depth = position + side * (chips - 1 - 2 * position)
    return 2 * depth + side


def gather_kernel(n, slot_count, grads_ref, slot_ref, panels, codes_ref, scale_ref,
                  squares, ring_send, ring_recv, sib_send, sib_recv):
    chips = n // 2
    half = chips // 2
    rows = grads_ref.shape[0]
    me = lax.axis_index("wide")
    core = me % 2
    pos = ring_position(me // 2, chips)

    def device_at(position, which):
        return ring_chip(position % chips, chips) * 2 + which

    targets = (device_at(pos + 1, core), device_at(pos + chips - 1, core))
    sibling = me + 1 - 2 * core

    barrier = pltpu.get_barrier_semaphore()
    for peer in (*targets, sibling):
        pl.semaphore_signal(barrier, inc=1, device_id={"wide": peer}, device_id_type=MESH)

    mine = pl.ds(pl.multiple_of(me * rows, 16), rows)
    for p in range(NP):
        panels[p, mine, :P_SIZE] = grads_ref[:, p * P_SIZE:(p + 1) * P_SIZE]
        panels[p, mine, P_SIZE:] = jnp.zeros((rows, P_PAD - P_SIZE), jnp.bfloat16)

    def block(device, chunk):
        row = pl.multiple_of(device * rows, 16)
        return panels.at[pl.ds(chunk * CHUNK_PANELS, CHUNK_PANELS), pl.ds(row, rows), :]

    def owner(direction, hop, which):
        shift = chips - hop if direction == 0 else hop
        return device_at(pos + shift, which)

    def ring_copy(direction, hop, chunk):
        ref = block(owner(direction, hop, core), chunk)
        return pltpu.make_async_remote_copy(
            src_ref=ref, dst_ref=ref,
            send_sem=ring_send.at[direction, hop, chunk],
            recv_sem=ring_recv.at[direction, hop, chunk],
            device_id={"wide": targets[direction]}, device_id_type=MESH)

    def ring_arrival(direction, hop, chunk):
        ref = block(owner(direction, hop, core), chunk)
        return pltpu.make_async_remote_copy(
            src_ref=ref, dst_ref=ref,
            send_sem=ring_send.at[direction, hop - 1, chunk],
            recv_sem=ring_recv.at[direction, hop - 1, chunk],
            device_id={"wide": targets[direction]}, device_id_type=MESH)

    def sib_copy(direction, hop, chunk, which):
        ref = block(owner(direction, hop, which), chunk)
        return pltpu.make_async_remote_copy(
            src_ref=ref, dst_ref=ref,
            send_sem=sib_send.at[direction, hop, chunk],
            recv_sem=sib_recv.at[direction, hop, chunk],
            device_id={"wide": sibling}, device_id_type=MESH)

    def add_squares(device, chunk):
        row = pl.multiple_of(device * rows, 16)
        total = squares[...]
        for p in range(CHUNK_PANELS):
            values = panels[chunk * CHUNK_PANELS + p, pl.ds(row, rows), :].astype(jnp.float32)
            values = values * values
            for k in range(P_PAD // 128):
                total = total + values[:, k * 128:(k + 1) * 128]
        squares[...] = total

    def halves(direction):
        return range(CHUNKS // 2) if direction == 0 else range(CHUNKS // 2, CHUNKS)

    pl.semaphore_wait(barrier, 3)
    for chunk in range(CHUNKS):
        for direction in range(2):
            ring_copy(direction, 0, chunk).start()
    for chunk in range(CHUNKS):
        sib_copy(0, 0, chunk, core).start()

    squares[...] = jnp.zeros_like(squares)
    for chunk in range(CHUNKS):
        add_squares(me, chunk)
    lane = lax.broadcasted_iota(jnp.int32, (8, 128), 1) + me * slot_count
    codes = jnp.zeros((8, 128), jnp.int32)
    for t, (i, j) in enumerate(zip(*np.triu_indices(NP))):
        codes = jnp.where(lane == slot_ref[t], int(1 + i * NP + j), codes)
    codes_ref[...] = codes
    for chunk in range(CHUNKS):
        sib_copy(0, 0, chunk, 1 - core).wait_recv()
        add_squares(sibling, chunk)

    def drain_sibling(hop, chunk, direction):
        sib_copy(direction, hop, chunk, 1 - core).wait_recv()
        add_squares(owner(direction, hop, 1 - core), chunk)

    for hop in range(1, half + 1):
        for chunk in range(CHUNKS):
            for direction in range(2):
                if hop < half or chunk in halves(direction):
                    ring_arrival(direction, hop, chunk).wait_recv()
                    if hop + 1 < half or (hop + 1 == half and chunk in halves(direction)):
                        ring_copy(direction, hop, chunk).start()
                    sib_copy(direction, hop, chunk, core).start()
            for direction in range(2):
                if hop < half or chunk in halves(direction):
                    add_squares(owner(direction, hop, core), chunk)
                    if hop > 1:
                        drain_sibling(hop - 1, chunk, direction)
                elif hop > 1:
                    drain_sibling(hop - 1, chunk, direction)
    for direction in range(2):
        for chunk in halves(direction):
            drain_sibling(half, chunk, direction)

    scale_ref[...] = jnp.full((8, 128), FF / jnp.sum(squares[...]), jnp.float32)

    for chunk in range(CHUNKS):
        sib_copy(0, 0, chunk, core).wait_send()
    for hop in range(half + 1):
        for direction in range(2):
            for chunk in range(CHUNKS):
                if hop + 1 < half or (hop + 1 == half and chunk in halves(direction)):
                    ring_copy(direction, hop, chunk).wait_send()
                if 1 <= hop < half or (hop == half and chunk in halves(direction)):
                    sib_copy(direction, hop, chunk, core).wait_send()


def gather(grads, tile_slot, n, slot_count):
    rows = grads.shape[0]
    hops = n // 4 + 1
    vmem = pl.BlockSpec(memory_space=pltpu.VMEM)
    return pl.pallas_call(
        functools.partial(gather_kernel, n, slot_count),
        out_shape=[
            pltpu.VMEM((NP, n * rows, P_PAD), jnp.bfloat16),
            jax.ShapeDtypeStruct((8, 128), jnp.int32),
            jax.ShapeDtypeStruct((8, 128), jnp.float32),
        ],
        in_specs=[vmem, pl.BlockSpec(memory_space=pltpu.SMEM)],
        out_specs=[vmem, vmem, vmem],
        scratch_shapes=[
            pltpu.VMEM((rows, 128), jnp.float32),
            pltpu.SemaphoreType.DMA((2, hops, CHUNKS)),
            pltpu.SemaphoreType.DMA((2, hops, CHUNKS)),
            pltpu.SemaphoreType.DMA((2, hops, CHUNKS)),
            pltpu.SemaphoreType.DMA((2, hops, CHUNKS)),
        ],
        compiler_params=pltpu.CompilerParams(
            collective_id=0, has_side_effects=True, vmem_limit_bytes=20 * 2**20),
        name="gather_panels",
    )(grads, tile_slot)


def tile_kernel(codes_ref, panels, scale_ref, out_ref):
    code = codes_ref[0, pl.program_id(0)]
    step = pl.program_id(1)

    @pl.when(code == 0)
    def _():
        out_ref[...] = jnp.zeros_like(out_ref)

    @pl.when(code > 0)
    def _():
        left, right = (code - 1) // NP, (code - 1) % NP
        first = pl.multiple_of(step * ROW_BLOCK, ROW_BLOCK)
        gram = lax.dot_general(
            panels[left, :, pl.ds(first, ROW_BLOCK)], panels[right],
            (((0,), (0,)), ((), ())), preferred_element_type=jnp.float32)
        out_ref[0] = gram[:, :P_SIZE] * scale_ref[0, 0]

        @pl.when(left == right)
        def _():
            here = pl.ds(first, ROW_BLOCK)
            row = lax.broadcasted_iota(jnp.int32, (ROW_BLOCK, P_SIZE), 0) + first
            col = lax.broadcasted_iota(jnp.int32, (ROW_BLOCK, P_SIZE), 1)
            out_ref[0] = out_ref[0] + jnp.where(row == col, DAMPING, 0.0)


def make_tiles(codes, panels, scale, slot_count):
    vmem = pl.BlockSpec(memory_space=pltpu.VMEM)
    return pl.pallas_call(
        tile_kernel,
        out_shape=jax.ShapeDtypeStruct((slot_count, P_SIZE, P_SIZE), jnp.float32),
        grid_spec=pltpu.PrefetchScalarGridSpec(
            num_scalar_prefetch=1,
            grid=(slot_count, pl.cdiv(P_SIZE, ROW_BLOCK)),
            in_specs=[vmem, vmem],
            out_specs=pl.BlockSpec((1, ROW_BLOCK, P_SIZE), lambda s, r, codes: (s, r, 0)),
        ),
        compiler_params=pltpu.CompilerParams(vmem_limit_bytes=20 * 2**20),
        name="factor_tiles",
    )(codes, panels, scale)


def shards(grads, tile_slot):
    n = lax.axis_size("wide")
    slot_count = (TILES + n - 1) // n
    panels, codes, scale = gather(grads, tile_slot, n, slot_count)
    return make_tiles(codes, panels, scale, slot_count)


def solution(mesh):
    in_specs = (P(("parts", "wide"), None), P("parts"))
    out_specs = P(("parts", "wide"), None, None)
    return jax.shard_map(shards, mesh=mesh, in_specs=in_specs, out_specs=out_specs, check_vma=False)
```

time: 256 us -> 67 us (0.26)
  the two profiles are of different devices: /device:TPU:18 before, /device:TPU:1 now
where the time goes in v1:
time: 67 us; the launch traced here: 66.7 us
  Pallas kernels  65 us (97%)
  local copies, waits for them, and re-layouts  1.68 us (3%)
    pallas_call x1, Pallas kernels, gather(): pl.pallas_call(functools.partial(gather_kernel, n, slot_count), out_shape...  45.4 us
    pallas_call x1, Pallas kernels, make_tiles(): pl.pallas_call(tile_kernel, out_shape=jax.ShapeDtypeStruct((slot_count, P...  19.7 us
    unnamed x4, local copies, waits for them, and re-layouts  1.68 us

profile of v1, /device:TPU:1, one launch (start us, length us, event | category | flops | bytes accessed | tf_op | source)
XLA Modules:
  0.0 66.7 jit_solution(11436124948705169531)
XLA Ops:
  0.0 0.0 copy-start
  0.0 1.0 %copy-done = bf16[16,14784]{1,0:T(8,128)(2,1)S(1)} copy-done((bf16[16,14784]{1,0:T(8,128)(2,1)S(1)}, bf16[16,14784]{1,0:T(8,128)(2,1)}, u32[]{:S(2)}) %copy-start) | copy-done | bytes 473112
  1.0 0.0 copy-start.1
  1.0 0.7 copy-done.1
  1.7 45.4 %gather_panels.1 = (bf16[12,256,1280]{2,1,0:T(8,128)(2,1)S(1)}, s32[8,128]{1,0:T(8,128)S(1)}, f32[8,128]{1,0:T(8,128)S(1)}) custom-call(bf16[16,14784]{1,0:T(8,128)(2,1)S(1)} %copy-done, s32[78]{0:T(128)S(1)} %copy-done.1), custom_call_target="tpu_custom_call" | custom-call | tf_op jit(solution)/shard_map/gather_panels/pallas_call | solution.py:167
  47.1 19.7 %factor_tiles.1 = f32[5,1232,1232]{2,1,0:T(8,128)} custom-call(s32[8,128]{1,0:T(8,128)S(1)} %get-tuple-element.8.codes_ref, bf16[12,256,1280]{2,1,0:T(8,128)(2,1)S(1)} %get-tuple-element.9.panels, f32[8,128]{1,0:T(8,128)S(1)} %get-tuple-element.10.scale_ref), custom_call_target="tpu_custom_call" | custom-call | tf_op jit(solution)/shard_map/factor_tiles/pallas_call | solution.py:216
Async XLA Ops:
  0.0 1.0 %copy-start = (bf16[16,14784]{1,0:T(8,128)(2,1)S(1)}, bf16[16,14784]{1,0:T(8,128)(2,1)}, u32[]{:S(2)}) copy-start(bf16[16,14784]{1,0:T(8,128)(2,1)} %grads_ref.1) | copy-start | bytes 1419268
  1.0 0.7 copy-start.1

commit v2 on v1

--- a/solution.py
+++ b/solution.py
@@ -18,6 +18,8 @@
 CHUNKS = 4
 CHUNK_PANELS = NP // CHUNKS
 ROW_BLOCK = 256
+TILE_BUFFERS = 6
+VMEM_BYTES = 64 * 2**20
 MESH = pl.DeviceIdType.MESH
 
 
@@ -36,11 +38,15 @@
     return 2 * depth + side
 
 
-def gather_kernel(n, slot_count, grads_ref, slot_ref, panels, codes_ref, scale_ref,
-                  squares, ring_send, ring_recv, sib_send, sib_recv):
+def gather_kernel(n, slot_count, grads_hbm, slot_hbm, panels, codes_ref, scale_ref,
+                  grads_ref, slot_ref, squares, arg_sems, ring_send, ring_recv, sib_send, sib_recv):
     chips = n // 2
     half = chips // 2
     rows = grads_ref.shape[0]
+    fetch_grads = pltpu.make_async_copy(grads_hbm, grads_ref, arg_sems.at[0])
+    fetch_slots = pltpu.make_async_copy(slot_hbm, slot_ref, arg_sems.at[1])
+    fetch_grads.start()
+    fetch_slots.start()
     me = lax.axis_index("wide")
     core = me % 2
     pos = ring_position(me // 2, chips)
@@ -56,9 +62,6 @@
         pl.semaphore_signal(barrier, inc=1, device_id={"wide": peer}, device_id_type=MESH)
 
     mine = pl.ds(pl.multiple_of(me * rows, 16), rows)
-    for p in range(NP):
-        panels[p, mine, :P_SIZE] = grads_ref[:, p * P_SIZE:(p + 1) * P_SIZE]
-        panels[p, mine, P_SIZE:] = jnp.zeros((rows, P_PAD - P_SIZE), jnp.bfloat16)
 
     def block(device, chunk):
         row = pl.multiple_of(device * rows, 16)
@@ -105,8 +108,13 @@
     def halves(direction):
         return range(CHUNKS // 2) if direction == 0 else range(CHUNKS // 2, CHUNKS)
 
-    pl.semaphore_wait(barrier, 3)
-    for chunk in range(CHUNKS):
+    fetch_grads.wait()
+    for chunk in range(CHUNKS):
+        for p in range(chunk * CHUNK_PANELS, (chunk + 1) * CHUNK_PANELS):
+            panels[p, mine, :P_SIZE] = grads_ref[:, p * P_SIZE:(p + 1) * P_SIZE]
+            panels[p, mine, P_SIZE:] = jnp.zeros((rows, P_PAD - P_SIZE), jnp.bfloat16)
+        if chunk == 0:
+            pl.semaphore_wait(barrier, 3)
         for direction in range(2):
             ring_copy(direction, 0, chunk).start()
     for chunk in range(CHUNKS):
@@ -115,6 +123,7 @@
     squares[...] = jnp.zeros_like(squares)
     for chunk in range(CHUNKS):
         add_squares(me, chunk)
+    fetch_slots.wait()
     lane = lax.broadcasted_iota(jnp.int32, (8, 128), 1) + me * slot_count
     codes = jnp.zeros((8, 128), jnp.int32)
     for t, (i, j) in enumerate(zip(*np.triu_indices(NP))):
@@ -168,60 +177,77 @@
         functools.partial(gather_kernel, n, slot_count),
         out_shape=[
             pltpu.VMEM((NP, n * rows, P_PAD), jnp.bfloat16),
-            jax.ShapeDtypeStruct((8, 128), jnp.int32),
-            jax.ShapeDtypeStruct((8, 128), jnp.float32),
+            pltpu.VMEM((8, 128), jnp.int32),
+            pltpu.VMEM((8, 128), jnp.float32),
         ],
-        in_specs=[vmem, pl.BlockSpec(memory_space=pltpu.SMEM)],
+        in_specs=[pl.BlockSpec(memory_space=pltpu.HBM)] * 2,
         out_specs=[vmem, vmem, vmem],
         scratch_shapes=[
+            pltpu.VMEM(grads.shape, jnp.bfloat16),
+            pltpu.SMEM(tile_slot.shape, jnp.int32),
             pltpu.VMEM((rows, 128), jnp.float32),
+            pltpu.SemaphoreType.DMA((2,)),
             pltpu.SemaphoreType.DMA((2, hops, CHUNKS)),
             pltpu.SemaphoreType.DMA((2, hops, CHUNKS)),
             pltpu.SemaphoreType.DMA((2, hops, CHUNKS)),
             pltpu.SemaphoreType.DMA((2, hops, CHUNKS)),
         ],
         compiler_params=pltpu.CompilerParams(
-            collective_id=0, has_side_effects=True, vmem_limit_bytes=20 * 2**20),
+            collective_id=0, has_side_effects=True,
+            vmem_limit_bytes=VMEM_BYTES - 2 * NP * n * rows * P_PAD - 2**18),
         name="gather_panels",
     )(grads, tile_slot)
 
 
-def tile_kernel(codes_ref, panels, scale_ref, out_ref):
-    code = codes_ref[0, pl.program_id(0)]
-    step = pl.program_id(1)
-
-    @pl.when(code == 0)
-    def _():
-        out_ref[...] = jnp.zeros_like(out_ref)
-
-    @pl.when(code > 0)
-    def _():
-        left, right = (code - 1) // NP, (code - 1) % NP
-        first = pl.multiple_of(step * ROW_BLOCK, ROW_BLOCK)
-        gram = lax.dot_general(
-            panels[left, :, pl.ds(first, ROW_BLOCK)], panels[right],
-            (((0,), (0,)), ((), ())), preferred_element_type=jnp.float32)
-        out_ref[0] = gram[:, :P_SIZE] * scale_ref[0, 0]
-
-        @pl.when(left == right)
-        def _():
-            here = pl.ds(first, ROW_BLOCK)
-            row = lax.broadcasted_iota(jnp.int32, (ROW_BLOCK, P_SIZE), 0) + first
-            col = lax.broadcasted_iota(jnp.int32, (ROW_BLOCK, P_SIZE), 1)
-            out_ref[0] = out_ref[0] + jnp.where(row == col, DAMPING, 0.0)
+def tile_kernel(slot_count, codes_ref, panels, scale_ref, out, tiles, sems):
+    starts = list(range(0, P_SIZE, ROW_BLOCK))
+
+    def write(step):
+        slot, first = step // len(starts), starts[step % len(starts)]
+        rows = min(ROW_BLOCK, P_SIZE - first)
+        return pltpu.make_async_copy(
+            tiles.at[step % TILE_BUFFERS, :rows, :], out.at[slot, pl.ds(first, rows), :],
+            sems.at[step % TILE_BUFFERS])
+
+    for slot in range(slot_count):
+        code = codes_ref[0, slot]
+        tile = jnp.maximum(code - 1, 0)
+        left, right = tile // NP, tile % NP
+        scale = jnp.where(code > 0, scale_ref[0, 0], 0.0)
+        damping = jnp.where(jnp.logical_and(left == right, code > 0), DAMPING, 0.0)
+        for block, first in enumerate(starts):
+            rows = min(ROW_BLOCK, P_SIZE - first)
+            step = slot * len(starts) + block
+            buffer = step % TILE_BUFFERS
+            if step >= TILE_BUFFERS:
+                write(step - TILE_BUFFERS).wait()
+            gram = lax.dot_general(
+                panels[left, :, first:first + ROW_BLOCK], panels[right],
+                (((0,), (0,)), ((), ())), preferred_element_type=jnp.float32)
+            factor = gram[:rows, :P_SIZE] * scale
+            tiles[buffer, :rows, :] = factor
+            last = min(first + ROW_BLOCK, P_SIZE)
+            row = lax.broadcasted_iota(jnp.int32, (rows, last - first), 0)
+            col = lax.broadcasted_iota(jnp.int32, (rows, last - first), 1)
+            tiles[buffer, :rows, first:last] = (
+                factor[:, first:last] + jnp.where(row == col, damping, 0.0))
+            write(step).start()
+    steps = slot_count * len(starts)
+    for step in range(max(0, steps - TILE_BUFFERS), steps):
+        write(step).wait()
 
 
 def make_tiles(codes, panels, scale, slot_count):
     vmem = pl.BlockSpec(memory_space=pltpu.VMEM)
     return pl.pallas_call(
-        tile_kernel,
+        functools.partial(tile_kernel, slot_count),
         out_shape=jax.ShapeDtypeStruct((slot_count, P_SIZE, P_SIZE), jnp.float32),
-        grid_spec=pltpu.PrefetchScalarGridSpec(
-            num_scalar_prefetch=1,
-            grid=(slot_count, pl.cdiv(P_SIZE, ROW_BLOCK)),
-            in_specs=[vmem, vmem],
-            out_specs=pl.BlockSpec((1, ROW_BLOCK, P_SIZE), lambda s, r, codes: (s, r, 0)),
-        ),
+        in_specs=[pl.BlockSpec(memory_space=pltpu.SMEM), vmem, vmem],
+        out_specs=pl.BlockSpec(memory_space=pl.ANY),
+        scratch_shapes=[
+            pltpu.VMEM((TILE_BUFFERS, ROW_BLOCK, P_SIZE), jnp.float32),
+            pltpu.SemaphoreType.DMA((TILE_BUFFERS,)),
+        ],
         compiler_params=pltpu.CompilerParams(vmem_limit_bytes=20 * 2**20),
         name="factor_tiles",
     )(codes, panels, scale)

time: 67 us -> 56.3 us (0.84)
  Pallas kernels: 65 us -> 56.1 us
  local copies, waits for them, and re-layouts: 1.68 us -> 0 us
    pallas_call x1, Pallas kernels: 19.7 us -> 11.3 us  [make_tiles(): pl.pallas_call(functools.partial(tile_kernel, slot_count), out_shape=jax....]
    unnamed x4 -> x0, local copies, waits for them, and re-layouts: 1.68 us -> none
where the time goes in v2:
time: 56.3 us; the launch traced here: 56.1 us
  Pallas kernels  56.1 us (100%)
    pallas_call x1, Pallas kernels, gather(): pl.pallas_call(functools.partial(gather_kernel, n, slot_count), out_shape...  44.8 us
    pallas_call x1, Pallas kernels, make_tiles(): pl.pallas_call(functools.partial(tile_kernel, slot_count), out_shape=jax....  11.3 us

profile of v2, /device:TPU:1, one launch (start us, length us, event | category | flops | bytes accessed | tf_op | source)
XLA Modules:
  0.0 56.1 jit_solution(13698094060912410487)
XLA Ops:
  0.0 44.8 %gather_panels.1 = (bf16[12,256,1280]{2,1,0:T(8,128)(2,1)S(1)}, s32[8,128]{1,0:T(8,128)S(1)}, f32[8,128]{1,0:T(8,128)S(1)}) custom-call(bf16[16,14784]{1,0:T(8,128)(2,1)} %grads_hbm.1, s32[78]{0:T(128)} %slot_hbm.1), custom_call_target="tpu_custom_call" | custom-call | tf_op jit(solution)/shard_map/gather_panels/pallas_call | solution.py:176
  44.8 11.3 %factor_tiles.1 = f32[5,1232,1232]{2,1,0:T(8,128)} custom-call(s32[8,128]{1,0:T(8,128)S(1)} %get-tuple-element.8.codes_ref, bf16[12,256,1280]{2,1,0:T(8,128)(2,1)S(1)} %get-tuple-element.9.panels, f32[8,128]{1,0:T(8,128)S(1)} %get-tuple-element.10.scale_ref), custom_call_target="tpu_custom_call" | custom-call | tf_op jit(solution)/shard_map/factor_tiles/pallas_call | solution.py:242

commit v3 on v2

--- a/solution.py
+++ b/solution.py
@@ -16,7 +16,7 @@
 
 P_PAD = 1280
 CHUNKS = 4
-CHUNK_PANELS = NP // CHUNKS
+CHUNK_COLS = 3712
 ROW_BLOCK = 256
 TILE_BUFFERS = 6
 VMEM_BYTES = 64 * 2**20
@@ -39,15 +39,16 @@
 
 
 def gather_kernel(n, slot_count, grads_hbm, slot_hbm, panels, codes_ref, scale_ref,
-                  grads_ref, slot_ref, squares, arg_sems, ring_send, ring_recv, sib_send, sib_recv):
+                  raw, slot_ref, squares, arg_sems, ring_send, ring_recv, sib_send, sib_recv):
     chips = n // 2
     half = chips // 2
-    rows = grads_ref.shape[0]
-    fetch_grads = pltpu.make_async_copy(grads_hbm, grads_ref, arg_sems.at[0])
+    rows = grads_hbm.shape[0]
+    me = lax.axis_index("wide")
+    mine = pl.ds(pl.multiple_of(me * rows, 16), rows)
+    fetch_grads = pltpu.make_async_copy(grads_hbm, raw.at[mine, :], arg_sems.at[0])
     fetch_slots = pltpu.make_async_copy(slot_hbm, slot_ref, arg_sems.at[1])
     fetch_grads.start()
     fetch_slots.start()
-    me = lax.axis_index("wide")
     core = me % 2
     pos = ring_position(me // 2, chips)
 
@@ -61,20 +62,26 @@
     for peer in (*targets, sibling):
         pl.semaphore_signal(barrier, inc=1, device_id={"wide": peer}, device_id_type=MESH)
 
-    mine = pl.ds(pl.multiple_of(me * rows, 16), rows)
+    def columns(chunk):
+        return chunk * CHUNK_COLS, min((chunk + 1) * CHUNK_COLS, FF)
 
     def block(device, chunk):
+        first, last = columns(chunk)
         row = pl.multiple_of(device * rows, 16)
-        return panels.at[pl.ds(chunk * CHUNK_PANELS, CHUNK_PANELS), pl.ds(row, rows), :]
+        return raw.at[pl.ds(row, rows), first:last]
+
+    def source(device, hop, chunk):
+        first, last = columns(chunk)
+        return block(device, chunk) if hop else grads_hbm.at[:, first:last]
 
     def owner(direction, hop, which):
         shift = chips - hop if direction == 0 else hop
         return device_at(pos + shift, which)
 
     def ring_copy(direction, hop, chunk):
-        ref = block(owner(direction, hop, core), chunk)
+        device = owner(direction, hop, core)
         return pltpu.make_async_remote_copy(
-            src_ref=ref, dst_ref=ref,
+            src_ref=source(device, hop, chunk), dst_ref=block(device, chunk),
             send_sem=ring_send.at[direction, hop, chunk],
             recv_sem=ring_recv.at[direction, hop, chunk],
             device_id={"wide": targets[direction]}, device_id_type=MESH)
@@ -88,41 +95,46 @@
             device_id={"wide": targets[direction]}, device_id_type=MESH)
 
     def sib_copy(direction, hop, chunk, which):
-        ref = block(owner(direction, hop, which), chunk)
+        device = owner(direction, hop, which)
         return pltpu.make_async_remote_copy(
-            src_ref=ref, dst_ref=ref,
+            src_ref=source(device, hop, chunk), dst_ref=block(device, chunk),
             send_sem=sib_send.at[direction, hop, chunk],
             recv_sem=sib_recv.at[direction, hop, chunk],
             device_id={"wide": sibling}, device_id_type=MESH)
 
-    def add_squares(device, chunk):
-        row = pl.multiple_of(device * rows, 16)
+    def take(device, chunk):
+        first, last = columns(chunk)
+        here = pl.ds(pl.multiple_of(device * rows, 16), rows)
+        for p in range(NP):
+            start, stop = max(p * P_SIZE, first), min((p + 1) * P_SIZE, last)
+            if start < stop:
+                panels[p, here, start - p * P_SIZE:stop - p * P_SIZE] = raw[here, start:stop]
+        whole = (last - first) // 128 * 128
+        values = raw[here, first:first + whole].astype(jnp.float32)
+        values = values * values
         total = squares[...]
-        for p in range(CHUNK_PANELS):
-            values = panels[chunk * CHUNK_PANELS + p, pl.ds(row, rows), :].astype(jnp.float32)
-            values = values * values
-            for k in range(P_PAD // 128):
-                total = total + values[:, k * 128:(k + 1) * 128]
+        for k in range(0, whole, 128):
+            total = total + values[:, k:k + 128]
         squares[...] = total
+        rest = last - first - whole
+        if rest:
+            values = raw[here, first + whole:last].astype(jnp.float32)
+            squares[:, :rest] = squares[:, :rest] + values * values
 
     def halves(direction):
         return range(CHUNKS // 2) if direction == 0 else range(CHUNKS // 2, CHUNKS)
 
-    fetch_grads.wait()
-    for chunk in range(CHUNKS):
-        for p in range(chunk * CHUNK_PANELS, (chunk + 1) * CHUNK_PANELS):
-            panels[p, mine, :P_SIZE] = grads_ref[:, p * P_SIZE:(p + 1) * P_SIZE]
-            panels[p, mine, P_SIZE:] = jnp.zeros((rows, P_PAD - P_SIZE), jnp.bfloat16)
-        if chunk == 0:
-            pl.semaphore_wait(barrier, 3)
+    pl.semaphore_wait(barrier, 3)
+    for chunk in range(CHUNKS):
         for direction in range(2):
             ring_copy(direction, 0, chunk).start()
     for chunk in range(CHUNKS):
         sib_copy(0, 0, chunk, core).start()
 
     squares[...] = jnp.zeros_like(squares)
-    for chunk in range(CHUNKS):
-        add_squares(me, chunk)
+    fetch_grads.wait()
+    for chunk in range(CHUNKS):
+        take(me, chunk)
     fetch_slots.wait()
     lane = lax.broadcasted_iota(jnp.int32, (8, 128), 1) + me * slot_count
     codes = jnp.zeros((8, 128), jnp.int32)
@@ -131,11 +143,11 @@
     codes_ref[...] = codes
     for chunk in range(CHUNKS):
         sib_copy(0, 0, chunk, 1 - core).wait_recv()
-        add_squares(sibling, chunk)
+        take(sibling, chunk)
 
     def drain_sibling(hop, chunk, direction):
         sib_copy(direction, hop, chunk, 1 - core).wait_recv()
-        add_squares(owner(direction, hop, 1 - core), chunk)
+        take(owner(direction, hop, 1 - core), chunk)
 
     for hop in range(1, half + 1):
         for chunk in range(CHUNKS):
@@ -147,7 +159,7 @@
                     sib_copy(direction, hop, chunk, core).start()
             for direction in range(2):
                 if hop < half or chunk in halves(direction):
-                    add_squares(owner(direction, hop, core), chunk)
+                    take(owner(direction, hop, core), chunk)
                     if hop > 1:
                         drain_sibling(hop - 1, chunk, direction)
                 elif hop > 1:
@@ -183,7 +195,7 @@
         in_specs=[pl.BlockSpec(memory_space=pltpu.HBM)] * 2,
         out_specs=[vmem, vmem, vmem],
         scratch_shapes=[
-            pltpu.VMEM(grads.shape, jnp.bfloat16),
+            pltpu.VMEM((n * rows, FF), jnp.bfloat16),
             pltpu.SMEM(tile_slot.shape, jnp.int32),
             pltpu.VMEM((rows, 128), jnp.float32),
             pltpu.SemaphoreType.DMA((2,)),

time: 56.3 us -> 55.4 us (0.984)
  Pallas kernels: 56.1 us -> 55.3 us
    pallas_call x1, Pallas kernels: 44.8 us -> 44 us  [gather(): pl.pallas_call(functools.partial(gather_kernel, n, slot_count), out_shape...]
where the time goes in v3:
time: 55.4 us; the launch traced here: 55.3 us
  Pallas kernels  55.3 us (100%)
    pallas_call x1, Pallas kernels, gather(): pl.pallas_call(functools.partial(gather_kernel, n, slot_count), out_shape...  44 us
    pallas_call x1, Pallas kernels, make_tiles(): pl.pallas_call(functools.partial(tile_kernel, slot_count), out_shape=jax....  11.3 us

profile of v3, /device:TPU:1, one launch (start us, length us, event | category | flops | bytes accessed | tf_op | source)
XLA Modules:
  0.0 55.3 jit_solution(15710410453343888543)
XLA Ops:
  0.0 44.0 %gather_panels.1 = (bf16[12,256,1280]{2,1,0:T(8,128)(2,1)S(1)}, s32[8,128]{1,0:T(8,128)S(1)}, f32[8,128]{1,0:T(8,128)S(1)}) custom-call(bf16[16,14784]{1,0:T(8,128)(2,1)} %grads_hbm.1, s32[78]{0:T(128)} %slot_hbm.1), custom_call_target="tpu_custom_call" | custom-call | tf_op jit(solution)/shard_map/gather_panels/pallas_call | solution.py:188
  44.0 11.3 %factor_tiles.1 = f32[5,1232,1232]{2,1,0:T(8,128)} custom-call(s32[8,128]{1,0:T(8,128)S(1)} %get-tuple-element.8.codes_ref, bf16[12,256,1280]{2,1,0:T(8,128)(2,1)S(1)} %get-tuple-element.9.panels, f32[8,128]{1,0:T(8,128)S(1)} %get-tuple-element.10.scale_ref), custom_call_target="tpu_custom_call" | custom-call | tf_op jit(solution)/shard_map/factor_tiles/pallas_call | solution.py:254
